TPU v7x, 256 devices: a whole 4x4x8 slice. The times are simulated.
256 devices in a mesh: req: 32 (over y, x, core), grp: 8 (over z).
Axes of the slice: x: 4, y: 4, z: 8, core: 2. Of those that a mesh axis runs over, the one named last changes fastest.
Arguments:
- queries: bfloat16 [4, 64, 8192], P(None, 'req', 'grp')
- cache_latents: bfloat16 [4, 65536, 4096], P(None, 'req', 'grp'), may hold values from -6 to 6
- fresh_latents: bfloat16 [4, 64, 4096], P(None, 'req', 'grp'), may hold values from -6 to 6
- lengths: int32 [4], replicated, may hold values from 1 to 65536, 163840 in all
- key_up: bfloat16 [8, 512, 128], P('grp'), may hold values from -0.25 to 0.25
- value_up: bfloat16 [8, 512, 128], P('grp'), may hold values from -0.25 to 0.25
- w_out: bfloat16 [8192, 8192], P('grp', 'req'), may hold values from -0.0625 to 0.0625
Outputs:
- projected: bfloat16 [256, 8192], P('grp', 'req')
Inputs may be any that keep to these rules, and one draw needn't show every extreme that they name: `lengths`: each request's cached length; one request uses all 65536 positions.
All inputs are finite; a program needn't handle non-finite values.
Results may differ from a plain program's by a relative error of at most 0.019.
The roundings to bfloat16 on the way count: a program that leaves them out, or rounds other values in their place, can miss the bound.
Values may be sent and summed in bfloat16 or wider, within the bound.
A program may use at most 128 MiB of HBM per device.

v0:
```python
import jax
import jax.numpy as jnp
from jax import lax
from jax.sharding import PartitionSpec as P

NEGATIVE = -1e30


def absorb_queries(queries, key_up):
    group_count, latent_rank, head_width = key_up.shape
    split_rows = queries.reshape(queries.shape[0], queries.shape[1], group_count, -1, head_width)
    latent = jnp.einsum("righa,gca->righc", split_rows, key_up, preferred_element_type=jnp.float32)
    return (latent * head_width ** (-0.5)).astype(jnp.bfloat16)


def partial_block(latent_q, latents, usable):
    scores = jnp.einsum("rihc,rpc->rihp", latent_q, latents, preferred_element_type=jnp.float32)
    usable_mask = usable[:, :, None, :]
    scores = jnp.where(usable_mask, scores, NEGATIVE)
    maxima = jnp.max(scores, axis=-1)
    weights = jnp.where(usable_mask, jnp.exp(scores - maxima[..., None]), 0.0)
    sums_exp = jnp.sum(weights, axis=-1)
    weighted = jnp.einsum(
        "rihp,rpc->rihc", weights.astype(jnp.bfloat16), latents, preferred_element_type=jnp.float32
    )
    return (maxima, sums_exp, weighted)


def to_heads(weighted, value_up):
    return jnp.einsum(
        "rigjc,gca->rigja", weighted, value_up.astype(jnp.float32), precision=lax.Precision.HIGHEST
    )


def on_device(queries, cache_latents, fresh_latents, lengths, key_up, value_up, w_out):
    num_reqs, own_rows = (queries.shape[0], queries.shape[1])
    device_idx = lax.axis_index("req")
    own_latent = absorb_queries(queries, key_up)
    all_latent, all_fresh = (
        lax.all_gather(own_latent, "req", axis=1, tiled=True),
        lax.all_gather(fresh_latents, "req", axis=1, tiled=True),
    )
    all_rows = all_latent.shape[1]
    extent = cache_latents.shape[1]
    positions = device_idx * extent + jnp.arange(extent, dtype=jnp.int32)
    usable = jnp.broadcast_to(
        positions[None, None, :] < lengths[:, None, None], (num_reqs, all_rows, extent)
    )
    row_ids = device_idx * own_rows + jnp.arange(own_rows, dtype=jnp.int32)
    fresh_usable = jnp.broadcast_to(
        jnp.arange(all_rows, dtype=jnp.int32)[None, :] <= row_ids[:, None],
        (num_reqs, own_rows, all_rows),
    )
    block_parts = [partial_block(all_latent[:, :, 0], cache_latents, usable)]
    fresh_parts = [partial_block(own_latent[:, :, 0], all_fresh, fresh_usable)]
    maxima = jnp.stack([entry[0] for entry in block_parts], axis=2)
    sums_exp = jnp.stack([entry[1] for entry in block_parts], axis=2)
    weighted = jnp.stack([entry[2] for entry in block_parts], axis=2)
    fresh_max = jnp.stack([entry[0] for entry in fresh_parts], axis=2)
    fresh_sums = jnp.stack([entry[1] for entry in fresh_parts], axis=2)
    fresh_weighted = jnp.stack([entry[2] for entry in fresh_parts], axis=2)
    got_max, got_sums, got_weighted = (
        lax.all_to_all(maxima[None], "req", split_axis=2, concat_axis=0, tiled=True),
        lax.all_to_all(sums_exp[None], "req", split_axis=2, concat_axis=0, tiled=True),
        lax.all_to_all(weighted[None], "req", split_axis=2, concat_axis=0, tiled=True),
    )
    highest = jnp.maximum(jnp.max(got_max, axis=0), fresh_max)
    block_scale = jnp.exp(got_max - highest)
    fresh_scale = jnp.exp(fresh_max - highest)
    total = jnp.sum(block_scale * got_sums, axis=0) + fresh_scale * fresh_sums
    combined = (
        jnp.sum(block_scale[..., None] * got_weighted, axis=0)
        + fresh_scale[..., None] * fresh_weighted
    )
    head_out = to_heads(combined / total[..., None], value_up)
    attention = head_out.astype(jnp.bfloat16).reshape(num_reqs, own_rows, -1)
    gathered = lax.all_gather(attention, "req", axis=1, tiled=True)
    flat_rows = gathered.reshape(-1, gathered.shape[2])
    return lax.psum_scatter(
        jnp.dot(flat_rows, w_out, preferred_element_type=jnp.float32).astype(jnp.bfloat16),
        "grp",
        scatter_dimension=0,
        tiled=True,
    )


def solution(mesh):
    return jax.shard_map(
        on_device,
        mesh=mesh,
        in_specs=(
            P(None, "req", "grp"),
            P(None, "req", "grp"),
            P(None, "req", "grp"),
            P(),
            P("grp", None, None),
            P("grp", None, None),
            P("grp", "req"),
        ),
        out_specs=P("grp", "req"),
        check_vma=False,
    )
```

profile of v0, /device:TPU:1, one launch (start us, length us, event | category | flops | bytes accessed | tf_op | source)
XLA Modules:
  0.0 253.6 jit_solution(14367137786337772358)
XLA Ops:
  6.5 0.0 copy-start
  6.5 0.0 all-gather.2.cloned.1.call-start
  6.5 0.8 reshape.168
  7.3 1.7 fusion.19
  9.0 0.0 all-gather.2.cloned.1.call-update
  9.1 0.7 broadcast_compare_fusion
  9.8 53.3 %all-gather.2.cloned.1.call-done = bf16[4,64,1,8,512]{4,3,1,0,2:T(8,128)(2,1)} async-done(((bf16[4,2,1,8,512]{4,3,1,0,2:T(8,128)(2,1)}), bf16[4,64,1,8,512]{4,3,1,0,2:T(8,128)(2,1)}) %all-gather.2.cloned.1.call-update) | async-done | bytes 2097168 | tf_op jit(solution)/shard_map/all_gather | solution.py:40
  63.1 14.3 %select_reduce_fusion = (f32[4,64,8]{2,1,0:T(8,128)S(1)}, f32[4,64,8,2048]{3,2,1,0:T(8,128)}) fusion(pred[4,2048]{1,0:T(4,128)(4,1)S(1)} %broadcast_compare_fusion, bf16[4,2048,512]{2,1,0:T(8,128)(2,1)} %param.8, bf16[4,64,1,8,512]{4,3,1,0,2:T(8,128)(2,1)} %all-gather.2.cloned.1.call-done), kind=kOutput, calls=%fused_computation.1 | convolution fusion | flops 4303353856 | bytes 27279360 | tf_op jit(solution)/shard_map/rihc,rpc->rihp/dot_general | solution.py:17
  77.4 0.7 copy.36
  78.1 5.1 %all-to-all-start = ((f32[1,4,64,1,8]{4,1,3,0,2:T(4,128)}), f32[1,4,64,1,8]{4,1,3,0,2:T(4,128)S(1)}, u32[]{:S(2)}, u32[]{:S(2)}) async-start(f32[1,4,64,1,8]{4,1,3,0,2:T(4,128)} %copy.36), calls=%async_computation | async-start | bytes 262144 | tf_op jit(solution)/shard_map/all_to_all | solution.py:63
  83.2 7.8 %fusion = f32[4,64,8]{2,1,0:T(8,128)S(1)} fusion(f32[4,64,8,2048]{3,2,1,0:T(8,128)} %get-tuple-element.8, f32[4,64,8]{2,1,0:T(8,128)S(1)} %get-tuple-element.7, pred[4,2048]{1,0:T(4,128)(4,1)S(1)} %broadcast_compare_fusion), kind=kLoop, calls=%fused_computation.2 | loop fusion | flops 16775168 | bytes 16801792 | tf_op jit(solution)/shard_map/reduce_sum | solution.py:22
  91.1 0.7 copy.45
  91.8 0.0 all-to-all-done
  91.8 7.4 %all-to-all-start.2 = ((f32[1,4,64,1,8]{4,1,3,0,2:T(4,128)}), f32[1,4,64,1,8]{4,1,3,0,2:T(4,128)S(1)}, u32[]{:S(2)}, u32[]{:S(2)}) async-start(f32[1,4,64,1,8]{4,1,3,0,2:T(4,128)} %copy.45), calls=%async_computation.2 | async-start | bytes 262144 | tf_op jit(solution)/shard_map/all_to_all | solution.py:64
  99.2 10.6 %fusion.11 = f32[1,4,64,1,8,512]{5,4,2,1,3,0:T(8,128)S(1)} fusion(bf16[4,2048,512]{2,1,0:T(8,128)(2,1)} %param.8, f32[4,64,8,2048]{3,2,1,0:T(8,128)} %get-tuple-element.8, f32[4,64,8]{2,1,0:T(8,128)S(1)} %get-tuple-element.7, pred[4,2048]{1,0:T(4,128)(4,1)S(1)} %broadcast_compare_fusion), kind=kOutput, calls=%fused_computation.13 | convolution fusion | flops 4311744512 | bytes 29376512 | tf_op jit(solution)/shard_map/rihp,rpc->rihc/dot_general | solution.py:23
  109.8 0.0 copy-start.3
  109.8 0.0 copy-start.1
  109.8 2.4 copy.40
  112.2 0.0 copy-start.2
  112.2 0.0 all-to-all-done.2
  112.2 7.6 %all-to-all-start.1 = ((f32[1,4,64,1,8,512]{5,4,1,3,0,2:T(8,128)}), f32[1,4,64,1,8,512]{5,4,1,3,0,2:T(8,128)}, u32[]{:S(2)}, u32[]{:S(2)}) async-start(f32[1,4,64,1,8,512]{5,4,1,3,0,2:T(8,128)} %copy.40), calls=%async_computation.1 | async-start | bytes 8388608 | tf_op jit(solution)/shard_map/all_to_all | solution.py:65
  119.8 0.0 reduce-scatter.2.cloned.1.call-start
  119.8 0.0 copy-done.3
  119.9 68.3 %all_gather.10 = bf16[4,64,512]{2,0,1:T(4,128)(2,1)S(1)} all-gather(bf16[4,2,512]{2,0,1:T(4,128)(2,1)S(1)} %copy.37), channel_id=1, replica_groups=mesh['req'=32,'grp'=8] {'req'}, dimensions={1}, use_global_device_ids=true | all-gather | bytes 270336 | tf_op jit(solution)/shard_map/all_gather | solution.py:41
  188.2 0.1 iota_compare_fusion
  188.3 0.0 copy-done.1
  188.3 0.3 fusion.36
  188.5 0.2 fusion.26
  188.7 0.1 reduce_max.28
  188.8 0.1 multiply_reduce_fusion.1
  188.9 0.0 all-to-all-done.1
  188.9 2.6 %multiply_reduce_fusion = f32[4,2,8,512]{3,2,0,1:T(8,128)S(1)} fusion(f32[32,4,2,1,8,512]{5,4,1,2,0,3:T(8,128)} %bitcast.20, f32[32,4,2,8]{3,1,2,0:T(4,128)S(1)} %bitcast.89), kind=kLoop, calls=%fused_computation.12 | loop fusion | flops 2064384 | bytes 4333568 | tf_op jit(solution)/shard_map/reduce_sum | solution.py:72
  191.5 0.2 fusion.18
  191.8 0.0 copy-done.2
  191.8 0.2 fusion.20
  192.0 24.1 %all_gather.11 = bf16[4,64,1024]{2,0,1:T(4,128)(2,1)S(1)} all-gather(bf16[4,2,1024]{2,0,1:T(4,128)(2,1)S(1)} %copy.48), channel_id=1, replica_groups=mesh['req'=32,'grp'=8] {'req'}, dimensions={1}, use_global_device_ids=true | all-gather | bytes 540672 | tf_op jit(solution)/shard_map/all_gather | solution.py:77
  216.1 0.2 copy.49
  216.3 0.0 copy-done
  216.3 0.9 convolution_convert_fusion
  217.2 0.0 reduce-scatter.2.cloned.1.call-update
  217.2 29.5 %reduce-scatter.2.cloned.1.call-done = bf16[32,256]{1,0:T(8,128)(2,1)} async-done(((bf16[256,256]{1,0:T(8,128)(2,1)}), bf16[32,256]{1,0:T(8,128)(2,1)}) %reduce-scatter.2.cloned.1.call-update) | async-done | bytes 16400 | tf_op jit(solution)/shard_map/reduce_scatter | solution.py:79
  (10 shorter events, 0.1 us)
Async XLA Ops:
  6.5 209.7 %copy-start = (bf16[1024,256]{1,0:T(8,128)(2,1)S(1)}, bf16[1024,256]{1,0:T(8,128)(2,1)}, u32[]{:S(2)}) copy-start(bf16[1024,256]{1,0:T(8,128)(2,1)} %param.13) | copy-start | bytes 1572868
  6.5 56.5 %all-gather.2.cloned.1.call-start = ((), (), s32[]{:S(2)}) async-start(), calls=%async_computation.4 | async-start | bytes 2162688 | tf_op jit(solution)/shard_map/all_gather | solution.py:40
  78.1 13.7 %all-to-all-start = ((f32[1,4,64,1,8]{4,1,3,0,2:T(4,128)}), f32[1,4,64,1,8]{4,1,3,0,2:T(4,128)S(1)}, u32[]{:S(2)}, u32[]{:S(2)}) async-start(f32[1,4,64,1,8]{4,1,3,0,2:T(4,128)} %copy.36), calls=%async_computation | async-start | bytes 262144 | tf_op jit(solution)/shard_map/all_to_all | solution.py:63
  91.8 20.4 %all-to-all-start.2 = ((f32[1,4,64,1,8]{4,1,3,0,2:T(4,128)}), f32[1,4,64,1,8]{4,1,3,0,2:T(4,128)S(1)}, u32[]{:S(2)}, u32[]{:S(2)}) async-start(f32[1,4,64,1,8]{4,1,3,0,2:T(4,128)} %copy.45), calls=%async_computation.2 | async-start | bytes 262144 | tf_op jit(solution)/shard_map/all_to_all | solution.py:64
  109.8 10.1 %copy-start.3 = (bf16[4,2,512]{2,1,0:T(2,128)(2,1)S(1)}, bf16[4,2,512]{2,1,0:T(2,128)(2,1)}, u32[]{:S(2)}) copy-start(bf16[4,2,512]{2,1,0:T(2,128)(2,1)} %param.9) | copy-start | bytes 24580
  109.8 78.5 %copy-start.1 = (bf16[512,4,2,8]{0,3,2,1:T(8,128)(2,1)S(1)}, bf16[512,4,2,8]{0,3,2,1:T(8,128)(2,1)}, u32[]{:S(2)}) copy-start(bf16[512,4,2,8]{0,3,2,1:T(8,128)(2,1)} %fusion.19) | copy-start | bytes 196612
  112.2 79.6 %copy-start.2 = (bf16[1,512,128]{2,1,0:T(8,128)(2,1)S(1)}, bf16[1,512,128]{2,1,0:T(8,128)(2,1)}, u32[]{:S(2)}) copy-start(bf16[1,512,128]{2,1,0:T(8,128)(2,1)} %param.12) | copy-start | bytes 393220
  112.2 76.7 %all-to-all-start.1 = ((f32[1,4,64,1,8,512]{5,4,1,3,0,2:T(8,128)}), f32[1,4,64,1,8,512]{5,4,1,3,0,2:T(8,128)}, u32[]{:S(2)}, u32[]{:S(2)}) async-start(f32[1,4,64,1,8,512]{5,4,1,3,0,2:T(8,128)} %copy.40), calls=%async_computation.1 | async-start | bytes 8388608 | tf_op jit(solution)/shard_map/all_to_all | solution.py:65
  119.8 126.9 %reduce-scatter.2.cloned.1.call-start = ((), (), s32[]{:S(2)}) async-start(), calls=%async_computation.5 | async-start | bytes 147456 | tf_op jit(solution)/shard_map/reduce_scatter | solution.py:79
Sparse Core Ops, SparseCore 0:
  10.0 53.0 all-gather.1
  217.4 29.3 reduce-scatter.1
where the time goes:
time: 259 us; the launch traced here: 254 us
  blocking collectives  92.4 us (36%)
  waiting for transfers between devices  82.8 us (32%)
  matrix products  28.2 us (11%)
  starting transfers between devices  20.1 us (8%)
  between operations  13.6 us (5%)
  other arithmetic  11.6 us (4%)
  local copies, waits for them, and re-layouts  4.87 us (2%)
    all_gather x1, blocking collectives, on_device(): lax.all_gather(fresh_latents, 'req', axis=1, tiled=True)  68.3 us
    all_gather x1, waiting for transfers between devices, on_device(): lax.all_gather(own_latent, 'req', axis=1, tiled=True)  53.3 us
    reduce_scatter x1, waiting for transfers between devices, on_device(): lax.psum_scatter(jnp.dot(flat_rows, w_out, preferred_element_type=jnp.flo...  29.5 us
    all_gather x1, blocking collectives, on_device(): gathered = lax.all_gather(attention, 'req', axis=1, tiled=True)  24.1 us
    dot_general x2, matrix products, partial_block(): jnp.einsum('rihc,rpc->rihp', latent_q, latents, preferred_element_type=jn...  14.6 us
    dot_general x2, matrix products, partial_block(): jnp.einsum('rihp,rpc->rihc', weights.astype(jnp.bfloat16), latents, prefe...  10.8 us
    reduce_sum x2, other arithmetic, partial_block(): sums_exp = jnp.sum(weights, axis=-1)  8.01 us
    all_to_all x1, starting transfers between devices, on_device(): lax.all_to_all(weighted[None], 'req', split_axis=2, concat_axis=0, tiled=...  7.57 us
  transfers between devices with their start and end apart: 5, of which 2 were waited for; matrix products, arithmetic and copies ran while one was open for 9% of the time, Pallas kernels for 0%

commit v1 on v0

v1 whole, which is shorter than its diff:
```python
import functools

import jax
import jax.numpy as jnp
from jax import lax
from jax.experimental import pallas as pl
from jax.experimental.pallas import tpu as pltpu
from jax.sharding import PartitionSpec as P

MESH = pl.DeviceIdType.MESH
NEGATIVE = -1e30

REQS = 4
PEERS = 32
GRPS = 8
HG = 8
HD = 128
RANK = 512
QN = 64
ROWS = QN * HG
EXTENT = 2048
OWN = ROWS // PEERS
CHUNK = 256
WIDE = 256


def dot_nt(a, b):
    return lax.dot_general(a, b, (((1,), (1,)), ((), ())), preferred_element_type=jnp.float32)


def dot_nn(a, b):
    return jnp.dot(a, b, preferred_element_type=jnp.float32)


def stat_rows(maxima, sums):
    n = maxima.shape[0] // OWN
    shape = (maxima.shape[0], 128)
    lane = lax.broadcasted_iota(jnp.int32, shape, 1)
    row = lax.rem(lax.broadcasted_iota(jnp.int32, shape, 0), OWN)
    spread = jnp.where(lane == row, maxima, jnp.where(lane == row + OWN, sums, 0.0))
    return jnp.sum(spread.reshape(n, OWN, 128), axis=1)


def kernel(
    len_ref, q_ref, f_ref, cache, ku_hbm, vu_hbm, wo_hbm, out_ref,
    held, ku, vu, wo,
    q_rows, q_send, q_all, q_wide, q_perm,
    f_rows, f_send, f_all, f_wide, f_keys,
    latent, o_send, o_all, s_send, s_all, f_out, f_stat,
    a_send, a_all, y_send, y_all,
    held_sem, w_sem, q_ssem, q_rsem, f_ssem, f_rsem, o_ssem, o_rsem, s_ssem, s_rsem,
    a_ssem, a_rsem, y_ssem, y_rsem,
):
    me = lax.axis_index("req")
    grp = lax.axis_index("grp")

    barrier = pltpu.get_barrier_semaphore()

    @pl.loop(1, PEERS)
    def _(j):
        pl.semaphore_signal(barrier, inc=1, device_id=(lax.rem(me + j, PEERS), grp), device_id_type=MESH)

    @pl.loop(1, GRPS)
    def _(j):
        pl.semaphore_signal(barrier, inc=1, device_id=(me, lax.rem(grp + j, GRPS)), device_id_type=MESH)

    def fetch_weights(i):
        return pltpu.make_async_copy((ku_hbm, vu_hbm, wo_hbm)[i], (ku, vu, wo)[i], w_sem.at[i])

    def fetch_cache(r):
        return pltpu.make_async_copy(cache.at[r], held.at[r], held_sem.at[r])

    fetch_weights(0).start()

    @pl.loop(0, REQS)
    def _(r):
        fetch_cache(r).start()

    fetch_weights(1).start()
    fetch_weights(2).start()

    for r in range(REQS):
        wide = q_ref[r].astype(jnp.float32)
        for i in range(2):
            for h in range(HG):
                q_rows[pl.ds(r * OWN + i * HG + h, 1), :] = wide[i:i + 1, h * HD:(h + 1) * HD]
        fresh = f_ref[r].astype(jnp.float32)
        for i in range(2):
            for c in range(4):
                f_rows[pl.ds(i * 16 + r * 4 + c, 1), :] = fresh[i:i + 1, c * 128:(c + 1) * 128]
    q_send[...] = q_rows[...].astype(jnp.bfloat16).reshape(REQS, OWN, HD)
    f_send[...] = f_rows[...].astype(jnp.bfloat16)

    pl.semaphore_wait(barrier, PEERS - 1 + GRPS - 1)

    def send_all(src, dst, send_sem, recv_sem):
        @pl.loop(0, PEERS - 1)
        def _(j):
            peer = lax.rem(me + 1 + lax.rem(j + 16, PEERS - 1), PEERS)
            pltpu.make_async_remote_copy(
                src_ref=src, dst_ref=dst, send_sem=send_sem, recv_sem=recv_sem,
                device_id=(peer, grp), device_id_type=MESH,
            ).start()
        pltpu.make_async_copy(src, dst, recv_sem).start()

    @pl.loop(0, REQS)
    def _(r):
        send_all(q_send.at[r], q_all.at[r, me], q_ssem.at[r], q_rsem.at[r])

    send_all(f_send, f_all.at[me], f_ssem, f_rsem)
    fetch_weights(0).wait()
    fetch_weights(1).wait()

    @pl.loop(0, REQS)
    def _(r):
        pltpu.make_async_copy(q_all.at[r], q_all.at[r], q_rsem.at[r]).wait()
        q_wide[...] = q_all[r].reshape(ROWS, HD).astype(jnp.float32)
        for h in range(HG):
            q_perm[h * QN:(h + 1) * QN, :] = q_wide[pl.ds(h, QN, stride=HG), :].astype(jnp.bfloat16)
        latent[r] = (dot_nt(q_perm[...], ku[...]) * HD ** (-0.5)).astype(jnp.bfloat16)
        fetch_cache(r).wait()
        position = me * EXTENT + lax.broadcasted_iota(jnp.int32, (1, EXTENT), 1)
        bias = jnp.where(position < len_ref[r], 0.0, -jnp.inf)
        for c in range(ROWS // CHUNK):
            rows = slice(c * CHUNK, (c + 1) * CHUNK)
            scores = dot_nt(latent[r, rows, :], held[r]) + bias
            maxima = jnp.maximum(jnp.max(scores, axis=1, keepdims=True), NEGATIVE)
            weights = jnp.exp(scores - maxima)
            sums = jnp.sum(weights, axis=1, keepdims=True)
            weighted = dot_nn(weights.astype(jnp.bfloat16), held[r])
            headed = dot_nn(weighted.astype(jnp.bfloat16), vu[...])
            owners = slice(c * CHUNK // OWN, (c + 1) * CHUNK // OWN)
            o_send[r, owners] = headed.astype(jnp.bfloat16).reshape(CHUNK // OWN, OWN, HD)
            s_send[r, owners, 0, :] = stat_rows(maxima, sums)

        @pl.loop(0, PEERS - 1)
        def _(j):
            peer = lax.rem(me + 1 + lax.rem(j + 16, PEERS - 1), PEERS)
            pltpu.make_async_remote_copy(
                src_ref=o_send.at[r, peer], dst_ref=o_all.at[r, me], send_sem=o_ssem.at[r], recv_sem=o_rsem.at[r],
                device_id=(peer, grp), device_id_type=MESH,
            ).start()
            pltpu.make_async_remote_copy(
                src_ref=s_send.at[r, peer], dst_ref=s_all.at[r, me], send_sem=s_ssem.at[r], recv_sem=s_rsem.at[r],
                device_id=(peer, grp), device_id_type=MESH,
            ).start()
        pltpu.make_async_copy(o_send.at[r, me], o_all.at[r, me], o_rsem.at[r]).start()
        pltpu.make_async_copy(s_send.at[r, me], s_all.at[r, me], s_rsem.at[r]).start()

    pltpu.make_async_copy(f_all, f_all, f_rsem).wait()
    f_wide[...] = f_all[...].astype(jnp.float32).reshape(QN * 16, 128)
    first = lax.rem(me, QN // OWN) * OWN

    @pl.loop(0, REQS)
    def _(r):
        for c in range(4):
            f_keys[:, c * 128:(c + 1) * 128] = f_wide[pl.ds(r * 4 + c, QN, stride=16), :].astype(jnp.bfloat16)
        own = latent[r, pl.ds(pl.multiple_of(me * OWN, OWN), OWN), :]
        scores = dot_nt(own, f_keys[...])
        row = first + lax.broadcasted_iota(jnp.int32, (OWN, QN), 0)
        usable = lax.broadcasted_iota(jnp.int32, (OWN, QN), 1) <= row
        scores = jnp.where(usable, scores, NEGATIVE)
        maxima = jnp.max(scores, axis=1, keepdims=True)
        weights = jnp.where(usable, jnp.exp(scores - maxima), 0.0)
        sums = jnp.sum(weights, axis=1, keepdims=True)
        weighted = dot_nn(weights.astype(jnp.bfloat16), f_keys[...])
        f_out[r] = dot_nn(weighted.astype(jnp.bfloat16), vu[...])
        f_stat[r] = stat_rows(maxima, sums)

    diagonal = lax.broadcasted_iota(jnp.int32, (OWN, 128), 0) == lax.broadcasted_iota(jnp.int32, (OWN, 128), 1)
    head_at = pl.ds(pl.multiple_of(me // (QN // OWN) * HD, HD), HD)
    row_at = pl.ds(pl.multiple_of(first, OWN), OWN)

    @pl.loop(0, REQS)
    def _(r):
        pltpu.make_async_copy(s_all.at[r], s_all.at[r], s_rsem.at[r]).wait()
        stats = s_all[r, :, 0, :]
        own_stat = f_stat[r]
        highest = jnp.maximum(jnp.max(stats, axis=0, keepdims=True), own_stat)
        scale = jnp.exp(stats - highest)
        own_scale = jnp.exp(own_stat - highest)
        total = jnp.sum(scale * pltpu.roll(stats, 128 - OWN, 1), axis=0, keepdims=True)
        total = total + own_scale * pltpu.roll(jnp.broadcast_to(own_stat, (8, 128)), 128 - OWN, 1)[:1]
        share = scale / total
        own_share = own_scale / total
        column = jnp.sum(jnp.where(diagonal[None], share[:, None, :], 0.0), axis=2, keepdims=True)
        own_column = jnp.sum(jnp.where(diagonal, own_share, 0.0), axis=1, keepdims=True)
        pltpu.make_async_copy(o_all.at[r], o_all.at[r], o_rsem.at[r]).wait()
        heads = jnp.sum(column * o_all[r].astype(jnp.float32), axis=0) + own_column * f_out[r]
        a_send[r] = heads.astype(jnp.bfloat16)
        send_all(a_send.at[r], a_all.at[r, row_at, head_at], a_ssem.at[r], a_rsem.at[r])

    fetch_weights(2).wait()

    @pl.loop(0, REQS)
    def _(r):
        pltpu.make_async_copy(a_all.at[r], a_all.at[r], a_rsem.at[r]).wait()
        y_send[r] = dot_nn(a_all[r], wo[...]).astype(jnp.bfloat16).reshape(2, QN // 2, WIDE)
        for half in range(2):
            @pl.when(r * 2 + half != grp)
            def _():
                pltpu.make_async_remote_copy(
                    src_ref=y_send.at[r, half], dst_ref=y_all.at[grp], send_sem=y_ssem, recv_sem=y_rsem,
                    device_id=(me, r * 2 + half), device_id_type=MESH,
                ).start()

            @pl.when(r * 2 + half == grp)
            def _():
                pltpu.make_async_copy(y_send.at[r, half], y_all.at[grp], y_rsem).start()

    pltpu.make_async_copy(y_all, y_all, y_rsem).wait()
    out_ref[...] = jnp.sum(y_all[...].astype(jnp.float32), axis=0).astype(jnp.bfloat16)

    others = pl.ds(0, PEERS - 1)

    @pl.loop(0, REQS)
    def _(r):
        for buffer, sem in ((q_all, q_ssem), (o_all, o_ssem), (s_all, s_ssem), (q_all, a_ssem)):
            pltpu.make_async_copy(buffer.at[r, others], buffer.at[r, others], sem.at[r]).wait()

    pltpu.make_async_copy(f_all.at[others], f_all.at[others], f_ssem).wait()
    pltpu.make_async_copy(y_all.at[pl.ds(0, GRPS - 1)], y_all.at[pl.ds(0, GRPS - 1)], y_ssem).wait()


def on_device(lengths, queries, fresh_latents, cache_latents, key_up, value_up, w_out):
    bf16, f32 = jnp.bfloat16, jnp.float32
    any_space = pl.BlockSpec(memory_space=pl.ANY)
    vmem = pl.BlockSpec(memory_space=pltpu.VMEM)
    dma, dmas = pltpu.SemaphoreType.DMA, pltpu.SemaphoreType.DMA((REQS,))
    return pl.pallas_call(
        kernel,
        out_shape=jax.ShapeDtypeStruct((QN * REQS // GRPS, WIDE), bf16),
        in_specs=[pl.BlockSpec(memory_space=pltpu.SMEM), vmem, vmem] + [any_space] * 4,
        out_specs=vmem,
        scratch_shapes=[
            pltpu.VMEM((REQS, EXTENT, RANK), bf16),
            pltpu.VMEM((RANK, HD), bf16),
            pltpu.VMEM((RANK, HD), bf16),
            pltpu.VMEM((HG * HD, WIDE), bf16),
            pltpu.VMEM((REQS * OWN, HD), f32),
            pltpu.VMEM((REQS, OWN, HD), bf16),
            pltpu.VMEM((REQS, PEERS, OWN, HD), bf16),
            pltpu.VMEM((ROWS, HD), f32),
            pltpu.VMEM((ROWS, HD), bf16),
            pltpu.VMEM((REQS * 8, 128), f32),
            pltpu.VMEM((REQS * 8, 128), bf16),
            pltpu.VMEM((PEERS, REQS * 8, 128), bf16),
            pltpu.VMEM((QN * 16, 128), f32),
            pltpu.VMEM((QN, RANK), bf16),
            pltpu.VMEM((REQS, ROWS, RANK), bf16),
            pltpu.VMEM((REQS, PEERS, OWN, HD), bf16),
            pltpu.VMEM((REQS, PEERS, OWN, HD), bf16),
            pltpu.VMEM((REQS, PEERS, 1, 128), f32),
            pltpu.VMEM((REQS, PEERS, 1, 128), f32),
            pltpu.VMEM((REQS, OWN, HD), f32),
            pltpu.VMEM((REQS, 1, 128), f32),
            pltpu.VMEM((REQS, OWN, HD), bf16),
            pltpu.VMEM((REQS, QN, HG * HD), bf16),
            pltpu.VMEM((REQS, 2, QN // 2, WIDE), bf16),
            pltpu.VMEM((GRPS, QN // 2, WIDE), bf16),
            dmas, pltpu.SemaphoreType.DMA((3,)), dmas, dmas, dma, dma, dmas, dmas, dmas, dmas,
            dmas, dmas, dma, dma,
        ],
        compiler_params=pltpu.CompilerParams(
            collective_id=0, has_side_effects=True, vmem_limit_bytes=56 * 2 ** 20
        ),
    )(lengths, queries, fresh_latents, cache_latents, key_up, value_up, w_out)


def solution(mesh):
    def whole(queries, cache_latents, fresh_latents, lengths, key_up, value_up, w_out):
        return jax.shard_map(
            lambda q, c, f, n, k, v, w: on_device(
                n, q, f, c, k.reshape(RANK, HD), v.reshape(RANK, HD), w
            ),
            mesh=mesh,
            in_specs=(
                P(None, "req", "grp"),
                P(None, "req", "grp"),
                P(None, "req", "grp"),
                P(),
                P("grp", None, None),
                P("grp", None, None),
                P("grp", "req"),
            ),
            out_specs=P("grp", "req"),
            check_vma=False,
        )(queries, cache_latents, fresh_latents, lengths, key_up, value_up, w_out)

    return whole
```

time: 259 us -> 50.9 us (0.20); the launches traced: 254 us -> 50.6 us
  blocking collectives: 92.4 us -> 0 us
  waiting for transfers between devices: 82.8 us -> 0 us
  Pallas kernels: 0 us -> 49.2 us
  matrix products: 28.2 us -> 0 us
  starting transfers between devices: 20.1 us -> 0 us
  between operations: 13.6 us -> 0.01 us
  other arithmetic: 11.6 us -> 0 us
  local copies, waits for them, and re-layouts: 4.87 us -> 1.32 us
    all_gather x2 -> x0, blocking collectives: 92.4 us -> none  [the longest x1 68.3 us: on_device(): lax.all_gather(fresh_latents, 'req', axis=1, tiled=True)]
    all_gather x1 -> x0, waiting for transfers between devices: 53.3 us -> none  [on_device(): lax.all_gather(own_latent, 'req', axis=1, tiled=True)]
    pallas_call x0 -> x1, Pallas kernels: none -> 49.2 us  [on_device(): pl.pallas_call(kernel, out_shape=jax.ShapeDtypeStruct((QN * REQS // GRPS,...]
    reduce_scatter x1 -> x0, waiting for transfers between devices: 29.5 us -> none  [on_device(): lax.psum_scatter(jnp.dot(flat_rows, w_out, preferred_element_type=jnp.flo...]
    dot_general x7 -> x0, matrix products: 28.2 us -> none  [the longest x2 14.6 us: partial_block(): jnp.einsum('rihc,rpc->rihp', latent_q, latents, preferred_element_type=jn...]
    all_to_all x3 -> x0, starting transfers between devices: 20.1 us -> none  [the longest x1 7.57 us: on_device(): lax.all_to_all(weighted[None], 'req', split_axis=2, concat_axis=0, tiled=...]
    reduce_sum x4 -> x0, other arithmetic: 10.7 us -> none  [the longest x2 8.01 us: partial_block(): sums_exp = jnp.sum(weights, axis=-1)]
    another operation x4 -> x0, local copies, waits for them, and re-layouts: 4.67 us -> none  [the longest x1 2.41 us: on_device(): weighted[None]]
  transfers between devices with their start and end apart: 5 -> 0, of which waited for: 2 -> 0; matrix products, arithmetic and copies ran while one was open for 9% -> 0% of each run, Pallas kernels for 0% -> 0%
where the time goes in v1:
time: 50.9 us; the launch traced here: 50.6 us
  Pallas kernels  49.2 us (97%)
  local copies, waits for them, and re-layouts  1.32 us (3%)
    pallas_call x1, Pallas kernels, on_device(): pl.pallas_call(kernel, out_shape=jax.ShapeDtypeStruct((QN * REQS // GRPS,...  49.2 us
    unnamed x1, local copies, waits for them, and re-layouts  1.32 us

profile of v1, /device:TPU:1, one launch (start us, length us, event | category | flops | bytes accessed | tf_op | source)
XLA Modules:
  0.0 50.6 jit_solution(2990238457116869140)
XLA Ops:
  0.0 49.2 %shard_map.73 = bf16[32,256]{1,0:T(8,128)(2,1)} custom-call(s32[4]{0:T(128)} %len_ref.1, bf16[4,2,1024]{2,1,0:T(2,128)(2,1)} %q_ref.1, bf16[4,2,512]{2,1,0:T(2,128)(2,1)} %f_ref.1, bf16[4,2048,512]{2,1,0:T(8,128)(2,1)} %cache.1, bf16[512,128]{1,0:T(8,128)(2,1)} %bitcast.2, bf16[512,128]{1,0:T(8,128)(2,1)} %bitcast.3, bf16[1024,256]{1,0:T(8,128)(2,1)} %wo_hbm.1), custom_call_target="tpu_custom_call" | custom-call | tf_op jit(solution)/shard_map/pallas_call | solution.py:230
  49.2 1.3 %copy.9 = bf16[32,256]{1,0:T(8,128)(2,1)} copy(bf16[32,256]{1,0:T(8,128)(2,1)} %shard_map.73) | data formatting | bytes 32768

commit v2 on v1

v2 whole, which is shorter than its diff:
```python
import functools

import jax
import jax.numpy as jnp
from jax import lax
from jax.experimental import pallas as pl
from jax.experimental.pallas import tpu as pltpu
from jax.sharding import PartitionSpec as P

MESH = pl.DeviceIdType.MESH
NEGATIVE = -1e30

REQS = 4
PEERS = 32
GRPS = 8
HG = 8
HD = 128
RANK = 512
QN = 64
ROWS = QN * HG
EXTENT = 2048
OWN = ROWS // PEERS
CHUNK = 256
BLOCK = 1024
CHIPS = PEERS // 2
WIDE = 256


def dot_nt(a, b):
    return lax.dot_general(a, b, (((1,), (1,)), ((), ())), preferred_element_type=jnp.float32)


def dot_nn(a, b):
    return jnp.dot(a, b, preferred_element_type=jnp.float32)


def stat_rows(maxima, sums):
    n = maxima.shape[0] // OWN
    lane = lax.broadcasted_iota(jnp.int32, (OWN, 128), 1)
    row = lax.broadcasted_iota(jnp.int32, (OWN, 128), 0)
    sums = jnp.where((lane == row + OWN)[None], sums.reshape(n, OWN, 1), 0.0)
    return jnp.sum(jnp.where((lane == row)[None], maxima.reshape(n, OWN, 1), sums), axis=1)


def attend(queries, keys, bias):
    chunks, blocks = ROWS // CHUNK, EXTENT // BLOCK
    items = [(b, c) for b in range(blocks) for c in range(chunks)]

    def score(b, c):
        at = slice(b * BLOCK, (b + 1) * BLOCK)
        return dot_nt(queries[c * CHUNK:(c + 1) * CHUNK, :], keys[at, :]) + bias[:, at]

    parts = [None] * chunks
    ahead = score(*items[0])
    for k, (b, c) in enumerate(items):
        scores = ahead
        if k + 1 < len(items):
            ahead = score(*items[k + 1])
        maxima = jnp.maximum(jnp.max(scores, axis=1, keepdims=True), NEGATIVE)
        if parts[c] is not None:
            maxima = jnp.maximum(maxima, parts[c][0])
        weights = jnp.exp(scores - maxima)
        sums = jnp.sum(weights, axis=1, keepdims=True)
        weighted = dot_nn(weights.astype(jnp.bfloat16), keys[b * BLOCK:(b + 1) * BLOCK, :])
        if parts[c] is not None:
            scale = jnp.exp(parts[c][0] - maxima)
            sums = sums + scale * parts[c][1]
            weighted = weighted + scale * parts[c][2]
        parts[c] = (maxima, sums, weighted)
    return parts


def kernel(
    len_hbm, q_hbm, f_hbm, cache, ku_hbm, vu_hbm, wo_hbm, out_ref,
    len_ref, q_ref, f_ref, held, ku, vu, wo,
    q_rows, q_send, q_all, q_wide, q_perm,
    f_rows, f_send, f_all, f_wide, f_keys,
    latent, o_send, o_all, s_send, s_all, f_out, f_stat,
    a_send, a_all, y_send, y_all,
    held_sem, w_sem, q_ssem, q_rsem, f_ssem, f_rsem, o_ssem, o_rsem, s_ssem, s_rsem,
    a_ssem, a_rsem, y_ssem, y_rsem, p_ssem,
):
    me = lax.axis_index("req")
    grp = lax.axis_index("grp")
    chip, core = me // 2, lax.rem(me, 2)
    sibling = me + 1 - 2 * core
    def owned(peer):
        return peer // 4 * 4 + lax.rem(peer, 2) * 2 + lax.rem(peer // 2, 2)

    mine = owned(me)

    barrier = pltpu.get_barrier_semaphore()

    @pl.loop(1, PEERS, unroll=True)
    def _(j):
        pl.semaphore_signal(barrier, inc=1, device_id=(lax.rem(me + j, PEERS), grp), device_id_type=MESH)

    @pl.loop(1, GRPS, unroll=True)
    def _(j):
        pl.semaphore_signal(barrier, inc=1, device_id=(me, lax.rem(grp + j, GRPS)), device_id_type=MESH)

    def fetch_weights(i):
        sources, targets = (ku_hbm, vu_hbm, wo_hbm, q_hbm, f_hbm, len_hbm), (ku, vu, wo, q_ref, f_ref, len_ref)
        return pltpu.make_async_copy(sources[i], targets[i], w_sem.at[i])

    def fetch_cache(r):
        return pltpu.make_async_copy(cache.at[r], held.at[r], held_sem.at[r])

    for i in (3, 4, 5, 0, 1):
        fetch_weights(i).start()

    @pl.loop(0, REQS)
    def _(r):
        fetch_cache(r).start()

    fetch_weights(2).start()
    for i in (3, 4, 5):
        fetch_weights(i).wait()

    for r in range(REQS):
        wide = q_ref[r].astype(jnp.float32)
        for i in range(2):
            for h in range(HG):
                q_rows[pl.ds(r * OWN + i * HG + h, 1), :] = wide[i:i + 1, h * HD:(h + 1) * HD]
        fresh = f_ref[r].astype(jnp.float32)
        for i in range(2):
            for c in range(4):
                f_rows[pl.ds(i * 16 + r * 4 + c, 1), :] = fresh[i:i + 1, c * 128:(c + 1) * 128]
    q_send[...] = q_rows[...].astype(jnp.bfloat16).reshape(REQS, OWN, HD)
    f_send[...] = f_rows[...].astype(jnp.bfloat16)

    pl.semaphore_wait(barrier, PEERS - 1 + GRPS - 1)

    def remote(src, dst, send_sem, recv_sem, peer):
        return pltpu.make_async_remote_copy(
            src_ref=src, dst_ref=dst, send_sem=send_sem, recv_sem=recv_sem,
            device_id=(peer, grp), device_id_type=MESH,
        )

    def send_all(src, dst, send_sem, recv_sem):
        @pl.loop(0, PEERS - 1, unroll=True)
        def _(j):
            remote(src, dst, send_sem, recv_sem, lax.rem(me + 1 + lax.rem(j + 16, PEERS - 1), PEERS)).start()
        pltpu.make_async_copy(src, dst, recv_sem).start()

    def send_chips(src, dst, send_sem, recv_sem):
        @pl.loop(0, CHIPS - 1, unroll=True)
        def _(j):
            remote(src, dst, send_sem, recv_sem, lax.rem(me + 2 + 2 * lax.rem(j + 7, CHIPS - 1), PEERS)).start()
        pltpu.make_async_copy(src, dst, recv_sem).start()

    def pass_on(buffer, send_sem, recv_sem):
        pltpu.make_async_copy(buffer, buffer, recv_sem).wait()
        remote(buffer, buffer, send_sem, recv_sem, sibling).start()

    def await_all(buffer, sem):
        pltpu.make_async_copy(buffer, buffer, sem).wait()

    send_all(q_send.at[0], q_all.at[0, core, chip], q_ssem.at[0], q_rsem.at[0, core])

    @pl.loop(1, REQS)
    def _(r):
        send_chips(q_send.at[r], q_all.at[r, core, chip], q_ssem.at[r], q_rsem.at[r, core])

    fetch_weights(0).wait()
    fetch_weights(1).wait()
    await_all(q_all.at[0, core], q_rsem.at[0, core])

    @pl.loop(0, REQS)
    def _(r):
        await_all(q_all.at[r, 1 - core], q_rsem.at[r, 1 - core])
        for d in range(PEERS):
            q_wide[d * OWN:(d + 1) * OWN, :] = q_all[r, d % 2, d // 2].astype(jnp.float32)
        for h in range(HG):
            q_perm[h * QN:(h + 1) * QN, :] = q_wide[pl.ds(h, QN, stride=HG), :].astype(jnp.bfloat16)
        latent[r] = (dot_nt(q_perm[...], ku[...]) * HD ** (-0.5)).astype(jnp.bfloat16)

        @pl.when(r < REQS - 1)
        def _():
            pass_on(q_all.at[r + 1, core], p_ssem.at[0, r], q_rsem.at[r + 1, core])

        @pl.when(r == 0)
        def _():
            send_chips(f_send, f_all.at[core, chip], f_ssem, f_rsem.at[core])

        fetch_cache(r).wait()
        position = me * EXTENT + lax.broadcasted_iota(jnp.int32, (1, EXTENT), 1)
        bias = jnp.where(position < len_ref[r], 0.0, -jnp.inf)
        for c, (maxima, sums, weighted) in enumerate(attend(latent.at[r], held.at[r], bias)):
            headed = dot_nn(weighted.astype(jnp.bfloat16), vu[...])
            owners = slice(c * CHUNK // OWN, (c + 1) * CHUNK // OWN)
            o_send[r, owners] = headed.astype(jnp.bfloat16).reshape(CHUNK // OWN, OWN, HD)
            s_send[r, owners, 0, :] = stat_rows(maxima, sums)

        @pl.loop(0, PEERS - 1, unroll=True)
        def _(j):
            peer = lax.rem(me + 1 + lax.rem(j + 16, PEERS - 1), PEERS)
            block = owned(peer)
            remote(o_send.at[r, block], o_all.at[r, me], o_ssem.at[r], o_rsem.at[r], peer).start()
            remote(s_send.at[r, block], s_all.at[r, me], s_ssem.at[r], s_rsem.at[r], peer).start()
        pltpu.make_async_copy(o_send.at[r, mine], o_all.at[r, me], o_rsem.at[r]).start()
        pltpu.make_async_copy(s_send.at[r, mine], s_all.at[r, me], s_rsem.at[r]).start()

    pass_on(f_all.at[core], p_ssem.at[0, REQS - 1], f_rsem.at[core])
    await_all(f_all.at[1 - core], f_rsem.at[1 - core])
    for d in range(PEERS):
        f_wide[d * 32:(d + 1) * 32, :] = f_all[d % 2, d // 2].astype(jnp.float32)
    first = (core * 2 + lax.rem(chip, 2)) * OWN

    @pl.loop(0, REQS)
    def _(r):
        for c in range(4):
            f_keys[:, c * 128:(c + 1) * 128] = f_wide[pl.ds(r * 4 + c, QN, stride=16), :].astype(jnp.bfloat16)
        own = latent[r, pl.ds(pl.multiple_of(mine * OWN, OWN), OWN), :]
        scores = dot_nt(own, f_keys[...])
        row = first + lax.broadcasted_iota(jnp.int32, (OWN, QN), 0)
        usable = lax.broadcasted_iota(jnp.int32, (OWN, QN), 1) <= row
        scores = jnp.where(usable, scores, NEGATIVE)
        maxima = jnp.max(scores, axis=1, keepdims=True)
        weights = jnp.where(usable, jnp.exp(scores - maxima), 0.0)
        sums = jnp.sum(weights, axis=1, keepdims=True)
        weighted = dot_nn(weights.astype(jnp.bfloat16), f_keys[...])
        f_out[r] = dot_nn(weighted.astype(jnp.bfloat16), vu[...])
        f_stat[r] = stat_rows(maxima, sums)

    diagonal = lax.broadcasted_iota(jnp.int32, (OWN, 128), 0) == lax.broadcasted_iota(jnp.int32, (OWN, 128), 1)
    head_at = pl.ds(pl.multiple_of(chip // 2 * HD, HD), HD)
    row_at = pl.ds(pl.multiple_of(lax.rem(chip, 2) * OWN, OWN), OWN)

    @pl.loop(0, REQS)
    def _(r):
        pltpu.make_async_copy(s_all.at[r], s_all.at[r], s_rsem.at[r]).wait()
        stats = s_all[r, :, 0, :]
        own_stat = f_stat[r]
        highest = jnp.maximum(jnp.max(stats, axis=0, keepdims=True), own_stat)
        scale = jnp.exp(stats - highest)
        own_scale = jnp.exp(own_stat - highest)
        total = jnp.sum(scale * pltpu.roll(stats, 128 - OWN, 1), axis=0, keepdims=True)
        total = total + own_scale * pltpu.roll(jnp.broadcast_to(own_stat, (8, 128)), 128 - OWN, 1)[:1]
        share = scale / total
        own_share = own_scale / total
        column = jnp.sum(jnp.where(diagonal[None], share[:, None, :], 0.0), axis=2, keepdims=True)
        own_column = jnp.sum(jnp.where(diagonal, own_share, 0.0), axis=1, keepdims=True)
        pltpu.make_async_copy(o_all.at[r], o_all.at[r], o_rsem.at[r]).wait()
        heads = jnp.sum(column * o_all[r].astype(jnp.float32), axis=0) + own_column * f_out[r]
        a_send[r] = heads.astype(jnp.bfloat16)
        own_block = a_all.at[r, core, row_at, head_at]

        @pl.when(r < REQS - 1)
        def _():
            send_chips(a_send.at[r], own_block, a_ssem.at[r], a_rsem.at[r, core])

        @pl.when(r == REQS - 1)
        def _():
            send_all(a_send.at[r], own_block, a_ssem.at[r], a_rsem.at[r, core])

    @pl.loop(0, REQS - 1)
    def _(r):
        pass_on(a_all.at[r, core], p_ssem.at[1, r], a_rsem.at[r, core])

    fetch_weights(2).wait()

    @pl.loop(0, REQS)
    def _(r):
        @pl.when(r == REQS - 1)
        def _():
            await_all(a_all.at[r, core], a_rsem.at[r, core])

        await_all(a_all.at[r, 1 - core], a_rsem.at[r, 1 - core])
        product = dot_nn(a_all[r].reshape(QN, HG * HD), wo[...])
        y_send[r] = product.astype(jnp.bfloat16).reshape(2, QN // 2, WIDE)
        for half in range(2):
            @pl.when(r * 2 + half != grp)
            def _():
                pltpu.make_async_remote_copy(
                    src_ref=y_send.at[r, half], dst_ref=y_all.at[grp], send_sem=y_ssem, recv_sem=y_rsem,
                    device_id=(me, r * 2 + half), device_id_type=MESH,
                ).start()

            @pl.when(r * 2 + half == grp)
            def _():
                pltpu.make_async_copy(y_send.at[r, half], y_all.at[grp], y_rsem).start()

    others = pl.ds(0, PEERS - 1)
    chips = pl.ds(0, CHIPS - 1)

    @pl.loop(0, REQS)
    def _(r):
        await_all(o_all.at[r, others], o_ssem.at[r])
        await_all(s_all.at[r, others], s_ssem.at[r])

    await_all(o_all.at[0, others], q_ssem.at[0])
    await_all(o_all.at[0, others], a_ssem.at[REQS - 1])

    @pl.loop(0, REQS - 1)
    def _(r):
        await_all(q_all.at[0, 0, chips], q_ssem.at[r + 1])
        await_all(q_all.at[0, 0], p_ssem.at[0, r])
        await_all(q_all.at[0, 0, chips], a_ssem.at[r])
        await_all(q_all.at[0, 0], p_ssem.at[1, r])

    await_all(f_all.at[0, chips], f_ssem)
    await_all(f_all.at[0], p_ssem.at[0, REQS - 1])
    pltpu.make_async_copy(y_all, y_all, y_rsem).wait()
    out_ref[...] = jnp.sum(y_all[...].astype(jnp.float32), axis=0).astype(jnp.bfloat16)
    await_all(y_all.at[pl.ds(0, GRPS - 1)], y_ssem)


def on_device(lengths, queries, fresh_latents, cache_latents, key_up, value_up, w_out):
    bf16, f32 = jnp.bfloat16, jnp.float32
    any_space = pl.BlockSpec(memory_space=pl.ANY)
    vmem = pl.BlockSpec(memory_space=pltpu.VMEM)
    dma, dmas = pltpu.SemaphoreType.DMA, pltpu.SemaphoreType.DMA((REQS,))
    pairs = pltpu.SemaphoreType.DMA((REQS, 2))
    return pl.pallas_call(
        kernel,
        out_shape=jax.ShapeDtypeStruct((QN * REQS // GRPS, WIDE), bf16),
        in_specs=[any_space] * 7,
        out_specs=vmem,
        scratch_shapes=[
            pltpu.SMEM((REQS,), jnp.int32),
            pltpu.VMEM((REQS, 2, HG * HD), bf16),
            pltpu.VMEM((REQS, 2, RANK), bf16),
            pltpu.VMEM((REQS, EXTENT, RANK), bf16),
            pltpu.VMEM((RANK, HD), bf16),
            pltpu.VMEM((RANK, HD), bf16),
            pltpu.VMEM((HG * HD, WIDE), bf16),
            pltpu.VMEM((REQS * OWN, HD), f32),
            pltpu.VMEM((REQS, OWN, HD), bf16),
            pltpu.VMEM((REQS, 2, CHIPS, OWN, HD), bf16),
            pltpu.VMEM((ROWS, HD), f32),
            pltpu.VMEM((ROWS, HD), bf16),
            pltpu.VMEM((REQS * 8, 128), f32),
            pltpu.VMEM((REQS * 8, 128), bf16),
            pltpu.VMEM((2, CHIPS, REQS * 8, 128), bf16),
            pltpu.VMEM((QN * 16, 128), f32),
            pltpu.VMEM((QN, RANK), bf16),
            pltpu.VMEM((REQS, ROWS, RANK), bf16),
            pltpu.VMEM((REQS, PEERS, OWN, HD), bf16),
            pltpu.VMEM((REQS, PEERS, OWN, HD), bf16),
            pltpu.VMEM((REQS, PEERS, 1, 128), f32),
            pltpu.VMEM((REQS, PEERS, 1, 128), f32),
            pltpu.VMEM((REQS, OWN, HD), f32),
            pltpu.VMEM((REQS, 1, 128), f32),
            pltpu.VMEM((REQS, OWN, HD), bf16),
            pltpu.VMEM((REQS, 2, QN // 2, HG * HD), bf16),
            pltpu.VMEM((REQS, 2, QN // 2, WIDE), bf16),
            pltpu.VMEM((GRPS, QN // 2, WIDE), bf16),
            dmas, pltpu.SemaphoreType.DMA((6,)), dmas, pairs, dma, pltpu.SemaphoreType.DMA((2,)),
            dmas, dmas, dmas, dmas, dmas, pairs, dma, dma, pltpu.SemaphoreType.DMA((2, REQS)),
        ],
        compiler_params=pltpu.CompilerParams(
            collective_id=0, has_side_effects=True, vmem_limit_bytes=56 * 2 ** 20
        ),
    )(lengths, queries, fresh_latents, cache_latents, key_up, value_up, w_out)


def solution(mesh):
    def whole(queries, cache_latents, fresh_latents, lengths, key_up, value_up, w_out):
        return jax.shard_map(
            lambda q, c, f, n, k, v, w: on_device(
                n, q, f, c, k.reshape(RANK, HD), v.reshape(RANK, HD), w
            ),
            mesh=mesh,
            in_specs=(
                P(None, "req", "grp"),
                P(None, "req", "grp"),
                P(None, "req", "grp"),
                P(),
                P("grp", None, None),
                P("grp", None, None),
                P("grp", "req"),
            ),
            out_specs=P("grp", "req"),
            check_vma=False,
        )(queries, cache_latents, fresh_latents, lengths, key_up, value_up, w_out)

    return whole
```

time: 50.9 us -> 47.9 us (0.941)
  Pallas kernels: 49.2 us -> 46.3 us
    pallas_call x1, Pallas kernels: 49.2 us -> 46.3 us  [on_device(): pl.pallas_call(kernel, out_shape=jax.ShapeDtypeStruct((QN * REQS // GRPS,...]
where the time goes in v2:
time: 47.9 us; the launch traced here: 47.7 us
  Pallas kernels  46.3 us (97%)
  local copies, waits for them, and re-layouts  1.32 us (3%)
    pallas_call x1, Pallas kernels, on_device(): pl.pallas_call(kernel, out_shape=jax.ShapeDtypeStruct((QN * REQS // GRPS,...  46.3 us
    unnamed x1, local copies, waits for them, and re-layouts  1.32 us

profile of v2, /device:TPU:1, one launch (start us, length us, event | category | flops | bytes accessed | tf_op | source)
XLA Modules:
  0.0 47.7 jit_solution(8200529263723140902)
XLA Ops:
  0.0 46.3 %shard_map.73 = bf16[32,256]{1,0:T(8,128)(2,1)} custom-call(s32[4]{0:T(128)} %len_hbm.1, bf16[4,2,1024]{2,1,0:T(2,128)(2,1)} %q_hbm.1, bf16[4,2,512]{2,1,0:T(2,128)(2,1)} %f_hbm.1, bf16[4,2048,512]{2,1,0:T(8,128)(2,1)} %cache.1, bf16[512,128]{1,0:T(8,128)(2,1)} %bitcast.2, bf16[512,128]{1,0:T(8,128)(2,1)} %bitcast.3, bf16[1024,256]{1,0:T(8,128)(2,1)} %wo_hbm.1), custom_call_target="tpu_custom_call" | custom-call | tf_op jit(solution)/shard_map/pallas_call | solution.py:315
  46.4 1.3 %copy.9 = bf16[32,256]{1,0:T(8,128)(2,1)} copy(bf16[32,256]{1,0:T(8,128)(2,1)} %shard_map.73) | data formatting | bytes 32768
